TPU v7x, 512 devices: a whole 4x8x8 slice. The times are simulated.
512 devices in a mesh: tm: 16 (over y, core), space: 32 (over x, z).
Axes of the slice: x: 4, y: 8, z: 8, core: 2. Of those that a mesh axis runs over, the one named last changes fastest.
Arguments:
- coupling: bfloat16 [16, 2048, 2048], P('tm', 'space'), may hold values from -0.125 to 0.125
- arrow_link: float32 [16, 2048, 64], P('tm'), may hold values from -0.75 to 0.75
- local_cov: float32 [16, 2048, 2048], P('tm', 'space'), as said below
- boundary_cov: float32 [16, 2048, 2048], P('tm', 'space'), as said below
- boundary_arrow: float32 [16, 2048, 64], P('tm', 'space'), may hold values from -6 to 6
- fixed_cov: float32 [64, 64], replicated, as said below
Outputs:
- diag_blocks: float32 [16, 2048, 2048], P('tm', 'space')
- cross_blocks: float32 [16, 2048, 2048], P('tm', 'space')
- arrow_covs: float32 [16, 2048, 64], P('tm', 'space')
Inputs may be any that keep to these rules, and one draw needn't show every extreme that they name: `local_cov`: each block is symmetric. `boundary_cov`: each block is symmetric. `fixed_cov`: symmetric.
All inputs are finite; a program needn't handle non-finite values.
Results may differ from a plain program's by a relative error of at most 0.0003.
Values may be sent and summed in bfloat16 or wider, within the bound.
No kernel may reach another device: no remote copies, remote signals or barrier semaphores. Data moves between devices by JAX's collectives and lax.ppermute only.
A program may use at most 64 MiB of HBM per device.

v0:
```python
import jax
import jax.numpy as jnp
from jax import lax
from jax.sharding import PartitionSpec as P


def passed_along(block, axis, distance):
    devices = range(lax.axis_size(axis))
    route = [(i - distance, i) for i in devices if i - distance in devices]
    return lax.ppermute(block, axis, route)


def shards(coupling, arrow_link, local_cov, boundary_cov, boundary_arrow, fixed_cov):
    highest = lax.Precision.HIGHEST
    next_block, next_arrow = passed_along((boundary_cov, boundary_arrow), "tm", -1)
    panels = lax.all_gather(coupling, "space", axis=1, tiled=True)[0]
    groups = lax.axis_size("space")
    rows_here = coupling.shape[1]
    offset = lax.axis_index("space") * rows_here
    link_block = arrow_link[0]
    link_rows = lax.dynamic_slice_in_dim(link_block, offset, rows_here, 0)
    succ_rows = next_block[0]
    succ_arrow = next_arrow[0]
    gathered = lax.all_gather(succ_arrow, "space", axis=0, tiled=True)
    carried = jnp.dot(coupling[0], gathered, precision=highest, preferred_element_type=jnp.float32)
    arrow_rows = carried + jnp.dot(
        link_rows, fixed_cov, precision=highest, preferred_element_type=jnp.float32
    )
    cross_turned = jnp.dot(
        succ_rows, panels.T, precision=highest, preferred_element_type=jnp.float32
    )
    cross_turned = cross_turned + jnp.dot(
        succ_arrow, link_block.T, precision=highest, preferred_element_type=jnp.float32
    )
    pieces = (
        cross_turned.reshape(rows_here, groups, rows_here)
        .transpose(2, 1, 0)
        .reshape(rows_here, groups * rows_here)
    )
    cross_rows = lax.all_to_all(pieces, "space", split_axis=1, concat_axis=1, tiled=True)
    diag_rows = local_cov[0] + jnp.dot(
        cross_rows, panels.T, precision=highest, preferred_element_type=jnp.float32
    )
    diag_rows = diag_rows + jnp.dot(
        arrow_rows, link_block.T, precision=highest, preferred_element_type=jnp.float32
    )
    return (diag_rows[None], cross_rows[None], arrow_rows[None])


def solution(mesh):
    return jax.shard_map(
        shards,
        mesh=mesh,
        in_specs=(
            P("tm", "space", None),
            P("tm", None, None),
            P("tm", "space", None),
            P("tm", "space", None),
            P("tm", "space", None),
            P(),
        ),
        out_specs=(P("tm", "space", None), P("tm", "space", None), P("tm", "space", None)),
        check_vma=False,
    )
```

profile of v0, /device:TPU:8, one launch (start us, length us, event | category | flops | bytes accessed | tf_op | source)
XLA Modules:
  0.0 218.1 jit_solution(1109246769169374447)
XLA Ops:
  7.2 0.0 copy-start
  7.2 0.0 copy-start.1
  7.2 0.0 copy-start.4
  7.2 0.0 all-gather.3.cloned.1.call-start
  7.2 0.7 all-gather.3.cloned.1.call-update
  7.9 1.9 collective-permute-start
  9.9 7.8 %collective-permute-start.1 = (f32[1,64,64]{2,1,0:T(8,128)}, f32[1,64,64]{2,1,0:T(8,128)S(1)}, u32[]{:S(2)}, u32[]{:S(2)}) collective-permute-start(f32[1,64,64]{2,1,0:T(8,128)} %param.10), channel_id=1, source_target_pairs={{32,0},{64,32},{96,64},{128,96},{160,128},{192,160},{224,192},{256... | collective-permute-start | bytes 49160 | tf_op jit(solution)/shard_map/ppermute | solution.py:10
  17.7 1.9 collective-permute-done.1
  19.6 0.0 copy-done
  19.6 0.6 fusion.13
  20.2 0.0 collective-permute-done
  20.2 100.1 %all-gather.3.cloned.1.call-done = bf16[1,2048,2048]{2,1,0:T(8,128)(2,1)} async-done(((bf16[1,64,2048]{2,1,0:T(8,128)(2,1)}), bf16[1,2048,2048]{2,1,0:T(8,128)(2,1)}) %all-gather.3.cloned.1.call-update) | async-done | bytes 8388624 | tf_op jit(solution)/shard_map/all_gather | solution.py:16
  120.3 10.0 %fusion.5 = f32[64,2048]{1,0:T(8,128)S(1)} fusion(f32[64,2048]{1,0:T(8,128)S(1)} %fusion.13, bf16[1,2048,2048]{2,1,0:T(8,128)(2,1)} %all-gather.3.cloned.1.call-done, f32[1,64,2048]{2,1,0:T(8,128)S(1)} %collective-permute-done), kind=kOutput, calls=%fused_computation.6 | convolution fusion | flops 3221356544 | bytes 9961472 | tf_op jit(solution)/shard_map/dot_general | solution.py:29
  130.4 0.0 copy-start.2
  130.4 0.3 copy.16
  130.7 1.5 reshape.17
  132.2 5.4 %all-to-all-start = ((f32[32,1,4096]{2,1,0:T(1,128)}), f32[32,1,4096]{2,1,0:T(1,128)S(1)}, u32[]{:S(2)}, u32[]{:S(2)}) async-start(f32[32,1,4096]{2,1,0:T(1,128)} %reshape.17), calls=%async_computation | async-start | bytes 1048576 | tf_op jit(solution)/shard_map/all_to_all | solution.py:40
  137.6 0.0 copy-done.4
  137.6 0.3 fusion.17
  138.0 56.4 %all-gather = f32[1,2048,64]{2,1,0:T(8,128)S(1)} all-gather(f32[1,64,64]{2,1,0:T(8,128)S(1)} %collective-permute-done.1), channel_id=2, replica_groups=mesh['tm'=16,'space'=32] {'space'}, dimensions={1}, use_global_device_ids=true | all-gather | bytes 540672 | tf_op jit(solution)/shard_map/all_gather | solution.py:24
  194.3 0.0 copy-done.1
  194.3 0.5 convolution_add_fusion.1
  194.8 0.0 copy-start.3
  194.8 0.0 all-to-all-done
  194.8 0.5 broadcast
  195.3 1.9 reduce
  197.2 0.4 reshape.18
  197.7 0.6 copy.14
  198.3 0.4 all_to_all.7
  198.6 1.2 broadcast_in_dim.10
  199.8 0.0 copy-done.2
  199.8 10.0 %fusion.8 = f32[64,2048]{1,0:T(8,128)S(1)} fusion(f32[64,2048]{1,0:T(8,128)S(1)} %all_to_all.7, bf16[1,2048,2048]{2,1,0:T(8,128)(2,1)} %all-gather.3.cloned.1.call-done, f32[1,64,2048]{2,1,0:T(8,128)S(1)} %copy-done.2), kind=kOutput, calls=%fused_computation.7 | convolution fusion | flops 3221356544 | bytes 9961472 | tf_op jit(solution)/shard_map/dot_general | solution.py:41
  209.9 0.0 copy-done.3
  209.9 1.4 fusion.4
Async XLA Ops:
  7.2 12.4 %copy-start = (f32[1,2048,64]{1,2,0:T(8,128)S(1)}, f32[1,2048,64]{1,2,0:T(8,128)}, u32[]{:S(2)}) copy-start(f32[1,2048,64]{1,2,0:T(8,128)} %param.7) | copy-start | bytes 1572868
  7.2 187.1 %copy-start.1 = (bf16[1,64,2048]{2,1,0:T(8,128)(2,1)S(1)}, bf16[1,64,2048]{2,1,0:T(8,128)(2,1)}, u32[]{:S(2)}) copy-start(bf16[1,64,2048]{2,1,0:T(8,128)(2,1)} %param.6) | copy-start | bytes 786436
  7.2 130.4 %copy-start.4 = (f32[64,64]{1,0:T(8,128)S(1)}, f32[64,64]{1,0:T(8,128)}, u32[]{:S(2)}) copy-start(f32[64,64]{1,0:T(8,128)} %param.11) | copy-start | bytes 49156
  7.2 113.1 %all-gather.3.cloned.1.call-start = ((), (), s32[]{:S(2)}) async-start(), calls=%async_computation.1 | async-start | bytes 8650752 | tf_op jit(solution)/shard_map/all_gather | solution.py:16
  7.9 12.2 %collective-permute-start = (f32[1,64,2048]{2,1,0:T(8,128)}, f32[1,64,2048]{2,1,0:T(8,128)S(1)}, u32[]{:S(2)}, u32[]{:S(2)}) collective-permute-start(f32[1,64,2048]{2,1,0:T(8,128)} %param.9), channel_id=1, source_target_pairs={{32,0},{64,32},{96,64},{128,96},{160,128},{192,160},{224,192},{256... | collective-permute-start | bytes 1572872 | tf_op jit(solution)/shard_map/ppermute | solution.py:10
  9.9 9.7 %collective-permute-start.1 = (f32[1,64,64]{2,1,0:T(8,128)}, f32[1,64,64]{2,1,0:T(8,128)S(1)}, u32[]{:S(2)}, u32[]{:S(2)}) collective-permute-start(f32[1,64,64]{2,1,0:T(8,128)} %param.10), channel_id=1, source_target_pairs={{32,0},{64,32},{96,64},{128,96},{160,128},{192,160},{224,192},{256... | collective-permute-start | bytes 49160 | tf_op jit(solution)/shard_map/ppermute | solution.py:10
  130.4 69.4 %copy-start.2 = (f32[1,64,2048]{2,1,0:T(8,128)S(1)}, f32[1,64,2048]{2,1,0:T(8,128)}, u32[]{:S(2)}) copy-start(f32[1,64,2048]{2,1,0:T(8,128)} %param.8) | copy-start | bytes 1572868
  132.2 62.7 %all-to-all-start = ((f32[32,1,4096]{2,1,0:T(1,128)}), f32[32,1,4096]{2,1,0:T(1,128)S(1)}, u32[]{:S(2)}, u32[]{:S(2)}) async-start(f32[32,1,4096]{2,1,0:T(1,128)} %reshape.17), calls=%async_computation | async-start | bytes 1048576 | tf_op jit(solution)/shard_map/all_to_all | solution.py:40
  194.8 15.0 %copy-start.3 = (f32[64,64]{1,0:T(8,128)}, f32[64,64]{1,0:T(8,128)S(1)}, u32[]{:S(2)}) copy-start(f32[64,64]{1,0:T(8,128)S(1)} %convolution_add_fusion.1) | copy-start | bytes 49156
Sparse Core Ops, SparseCore 0:
  11.2 109.0 all-gather.2
where the time goes:
time: 218 us
  waiting for transfers between devices  103 us (47%)
  blocking collectives  56.4 us (26%)
  matrix products  22.8 us (10%)
  starting transfers between devices  15.2 us (7%)
  between operations  14.2 us (7%)
  local copies, waits for them, and re-layouts  4.86 us (2%)
    all_gather x1, waiting for transfers between devices, shards(): panels = lax.all_gather(coupling, 'space', axis=1, tiled=True)[0]  100 us
    all_gather x1, blocking collectives, shards(): gathered = lax.all_gather(succ_arrow, 'space', axis=0, tiled=True)  56.4 us
    dot_general x1, matrix products, shards(): jnp.dot(cross_rows, panels.T, precision=highest, preferred_element_type=j...  10 us
    dot_general x1, matrix products, shards(): jnp.dot(succ_rows, panels.T, precision=highest, preferred_element_type=jn...  10 us
    ppermute x2, starting transfers between devices, passed_along(): return lax.ppermute(block, axis, route)  9.75 us
    all_to_all x1, starting transfers between devices, shards(): lax.all_to_all(pieces, 'space', split_axis=1, concat_axis=1, tiled=True)  5.45 us
  transfers between devices with their start and end apart: 4, of which 2 were waited for; matrix products, arithmetic and copies ran while one was open for 1% of the time, Pallas kernels for 0%

commit v1 on v0

--- a/solution.py
+++ b/solution.py
@@ -2,6 +2,11 @@
 import jax.numpy as jnp
 from jax import lax
 from jax.sharding import PartitionSpec as P
+
+
+def gather_from_all(shard, axis, dim):
+    copies = jnp.concatenate([shard] * lax.axis_size(axis), axis=dim)
+    return lax.all_to_all(copies, axis, dim, dim, tiled=True)
 
 
 def passed_along(block, axis, distance):
@@ -13,7 +18,7 @@
 def shards(coupling, arrow_link, local_cov, boundary_cov, boundary_arrow, fixed_cov):
     highest = lax.Precision.HIGHEST
     next_block, next_arrow = passed_along((boundary_cov, boundary_arrow), "tm", -1)
-    panels = lax.all_gather(coupling, "space", axis=1, tiled=True)[0]
+    panels = gather_from_all(coupling, "space", 1)[0]
     groups = lax.axis_size("space")
     rows_here = coupling.shape[1]
     offset = lax.axis_index("space") * rows_here

time: 218 us -> 480 us (2.20)
  the two profiles are of different devices: /device:TPU:8 before, /device:TPU:32 now
where the time goes in v1:
time: 480 us; the launch traced here: 478 us
  waiting for transfers between devices  184 us (38%)
  local copies, waits for them, and re-layouts  115 us (24%)
  blocking collectives  55.9 us (12%)
  other arithmetic  52.9 us (11%)
  matrix products  37.8 us (8%)
  starting transfers between devices  32 us (7%)
    all_to_all x1, waiting for transfers between devices, gather_from_all(): return lax.all_to_all(copies, axis, dim, dim, tiled=True)  179 us
    unnamed x50, local copies, waits for them, and re-layouts  63.3 us
    all_gather x1, blocking collectives, shards(): gathered = lax.all_gather(succ_arrow, 'space', axis=0, tiled=True)  55.9 us
    unnamed x1, other arithmetic  51 us
    concatenate x2, local copies, waits for them, and re-layouts, gather_from_all(): copies = jnp.concatenate([shard] * lax.axis_size(axis), axis=dim)  48.4 us
    dot_general x1, matrix products, shards(): jnp.dot(cross_rows, panels.T, precision=highest, preferred_element_type=j...  17.6 us
    dot_general x1, matrix products, shards(): jnp.dot(succ_rows, panels.T, precision=highest, preferred_element_type=jn...  17.5 us
    all_to_all x1, starting transfers between devices, shards(): lax.all_to_all(pieces, 'space', split_axis=1, concat_axis=1, tiled=True)  14 us
  transfers between devices with their start and end apart: 4, of which 2 were waited for; matrix products, arithmetic and copies ran while one was open for 5% of the time, Pallas kernels for 0%

profile of v1, /device:TPU:32, one launch (start us, length us, event | category | flops | bytes accessed | tf_op | source)
XLA Modules:
  0.0 477.9 jit_solution(16665585379537528735)
XLA Ops:
  0.6 0.0 copy-start
  0.6 0.0 copy-start.1
  0.7 1.0 constant_dynamic-update-slice_fusion.31
  1.7 1.0 constant_dynamic-update-slice_fusion.30
  2.7 1.0 constant_dynamic-update-slice_fusion.29
  3.6 1.0 constant_dynamic-update-slice_fusion.28
  4.6 1.0 constant_dynamic-update-slice_fusion.27
  5.6 1.0 constant_dynamic-update-slice_fusion.26
  6.6 1.0 constant_dynamic-update-slice_fusion.25
  7.5 1.0 constant_dynamic-update-slice_fusion.24
  8.5 1.0 constant_dynamic-update-slice_fusion.23
  9.5 1.0 constant_dynamic-update-slice_fusion.22
  10.5 1.0 constant_dynamic-update-slice_fusion.21
  11.4 1.0 constant_dynamic-update-slice_fusion.20
  12.4 1.0 constant_dynamic-update-slice_fusion.19
  13.4 1.0 constant_dynamic-update-slice_fusion.18
  14.3 1.0 constant_dynamic-update-slice_fusion.17
  15.3 1.0 constant_dynamic-update-slice_fusion.16
  16.3 0.0 copy-done.1
  16.7 48.3 %copy.101 = bf16[1,2048,2048]{2,0,1:T(2,128)(2,1)} copy(bf16[1,2048,2048]{2,1,0:T(8,128)(2,1)S(1)} %constant_dynamic-update-slice_fusion) | data formatting | bytes 16777216 | tf_op jit(solution)/shard_map/concatenate | solution.py:8
  65.1 0.5 broadcast
  65.6 51.0 %reduce = bf16[2048,2048]{1,0:T(8,128)(2,1)} reduce(bf16[2048,1,2048]{2,1,0:T(2,128)(2,1)} %bitcast.54, bf16[]{:T(256)} %broadcast), dimensions={1}, to_apply=%bitcast.51.reduce_sub_computation | reduce | bytes 16777218
  116.6 21.6 %reshape.17 = bf16[32,2,65536]{2,1,0:T(2,128)(2,1)} reshape(bf16[2048,2048]{1,0:T(8,128)(2,1)} %reduce) | data formatting | bytes 16777216
  138.2 0.0 copy-start.5
  138.2 0.0 copy-start.6
  138.2 13.4 %all-to-all-start = ((bf16[32,2,65536]{2,1,0:T(2,128)(2,1)}), bf16[32,2,65536]{2,1,0:T(2,128)(2,1)}, u32[]{:S(2)}, u32[]{:S(2)}) async-start(bf16[32,2,65536]{2,1,0:T(2,128)(2,1)} %reshape.17), calls=%async_computation | async-start | bytes 16777216 | tf_op jit(solution)/shard_map/all_to_all | solution.py:9
  151.7 0.0 copy-done.5
  151.7 1.9 collective-permute-start
  153.6 0.0 copy-done.6
  153.6 2.6 collective-permute-start.1
  156.3 4.4 collective-permute-done.1
  160.6 0.0 copy-done
  160.6 0.6 fusion.18
  161.2 179.3 %all-to-all-done = bf16[32,2,65536]{2,1,0:T(2,128)(2,1)} async-done(((bf16[32,2,65536]{2,1,0:T(2,128)(2,1)}), bf16[32,2,65536]{2,1,0:T(2,128)(2,1)}, u32[]{:S(2)}, u32[]{:S(2)}) %all-to-all-start) | async-done | bytes 8388640 | tf_op jit(solution)/shard_map/all_to_all | solution.py:9
  340.5 23.4 %reshape.18 = bf16[2048,1,2048]{2,1,0:T(2,128)(2,1)} reshape(bf16[32,2,65536]{2,1,0:T(2,128)(2,1)} %all-to-all-done) | data formatting | bytes 16777216
  363.9 0.0 copy-start.4
  363.9 0.0 collective-permute-done
  363.9 17.5 %fusion.10 = f32[64,2048]{1,0:T(8,128)S(1)} fusion(f32[64,2048]{1,0:T(8,128)S(1)} %fusion.18, bf16[1,2048,2048]{2,0,1:T(2,128)(2,1)} %bitcast.52, f32[1,64,2048]{2,1,0:T(8,128)S(1)} %collective-permute-done), kind=kOutput, calls=%fused_computation.9 | convolution fusion | flops 3221356544 | bytes 9961472 | tf_op jit(solution)/shard_map/dot_general | solution.py:34
  381.4 0.0 copy-start.2
  381.4 0.3 copy.84
  381.8 1.5 reshape.19
  383.2 14.0 %all-to-all-start.1 = ((f32[32,1,4096]{2,1,0:T(1,128)}), f32[32,1,4096]{2,1,0:T(1,128)S(1)}, u32[]{:S(2)}, u32[]{:S(2)}) async-start(f32[32,1,4096]{2,1,0:T(1,128)} %reshape.19), calls=%async_computation.1 | async-start | bytes 1048576 | tf_op jit(solution)/shard_map/all_to_all | solution.py:45
  397.2 0.0 copy-done.4
  397.2 0.3 fusion.22
  397.5 55.9 %all-gather = f32[1,2048,64]{2,1,0:T(8,128)S(1)} all-gather(f32[1,64,64]{2,1,0:T(8,128)S(1)} %collective-permute-done.1), channel_id=2, replica_groups=mesh['tm'=16,'space'=32] {'space'}, dimensions={1}, use_global_device_ids=true | all-gather | bytes 540672 | tf_op jit(solution)/shard_map/all_gather | solution.py:29
  453.5 0.5 convolution_add_fusion.1
  454.0 0.0 copy-start.3
  454.0 0.0 all-to-all-done.1
  454.0 0.5 broadcast.1
  454.5 1.9 reduce.1
  456.4 0.4 reshape.20
  456.8 0.6 copy.82
  457.4 0.4 all_to_all.11
  457.8 1.2 broadcast_in_dim.10
  459.0 0.0 copy-done.2
  459.0 17.6 %fusion.13 = f32[64,2048]{1,0:T(8,128)S(1)} fusion(f32[64,2048]{1,0:T(8,128)S(1)} %all_to_all.11, bf16[1,2048,2048]{2,0,1:T(2,128)(2,1)} %bitcast.53, f32[1,64,2048]{2,1,0:T(8,128)S(1)} %copy-done.2), kind=kOutput, calls=%fused_computation.10 | convolution fusion | flops 3221356544 | bytes 9961472 | tf_op jit(solution)/shard_map/dot_general | solution.py:46
  476.5 0.0 copy-done.3
  476.5 1.4 fusion.9
  (16 shorter events, 0.3 us)
Async XLA Ops:
  0.6 160.0 %copy-start = (f32[1,2048,64]{1,2,0:T(8,128)S(1)}, f32[1,2048,64]{1,2,0:T(8,128)}, u32[]{:S(2)}) copy-start(f32[1,2048,64]{1,2,0:T(8,128)} %param.7) | copy-start | bytes 1572868
  0.6 15.7 %copy-start.1 = (bf16[1,64,2048]{2,1,0:T(8,128)(2,1)S(1)}, bf16[1,64,2048]{2,1,0:T(8,128)(2,1)}, u32[]{:S(2)}) copy-start(bf16[1,64,2048]{2,1,0:T(8,128)(2,1)} %param.6) | copy-start | bytes 786436
  138.2 13.4 %copy-start.5 = (f32[1,64,2048]{2,1,0:T(8,128)S(1)}, f32[1,64,2048]{2,1,0:T(8,128)}, u32[]{:S(2)}) copy-start(f32[1,64,2048]{2,1,0:T(8,128)} %param.9) | copy-start | bytes 1572868
  138.2 15.4 %copy-start.6 = (f32[1,64,64]{2,1,0:T(8,128)S(1)}, f32[1,64,64]{2,1,0:T(8,128)}, u32[]{:S(2)}) copy-start(f32[1,64,64]{2,1,0:T(8,128)} %param.10) | copy-start | bytes 49156
  138.2 202.2 %all-to-all-start = ((bf16[32,2,65536]{2,1,0:T(2,128)(2,1)}), bf16[32,2,65536]{2,1,0:T(2,128)(2,1)}, u32[]{:S(2)}, u32[]{:S(2)}) async-start(bf16[32,2,65536]{2,1,0:T(2,128)(2,1)} %reshape.17), calls=%async_computation | async-start | bytes 16777216 | tf_op jit(solution)/shard_map/all_to_all | solution.py:9
  151.7 212.2 %collective-permute-start = (f32[1,64,2048]{2,1,0:T(8,128)S(1)}, f32[1,64,2048]{2,1,0:T(8,128)S(1)}, u32[]{:S(2)}, u32[]{:S(2)}) collective-permute-start(f32[1,64,2048]{2,1,0:T(8,128)S(1)} %copy-done.5), channel_id=1, source_target_pairs={{32,0},{64,32},{96,64},{128,96},{160,128},{192,160},{224,192},{256... | collective-permute-start | bytes 1572872 | tf_op jit(solution)/shard_map/ppermute | solution.py:15
  153.6 7.0 %collective-permute-start.1 = (f32[1,64,64]{2,1,0:T(8,128)S(1)}, f32[1,64,64]{2,1,0:T(8,128)S(1)}, u32[]{:S(2)}, u32[]{:S(2)}) collective-permute-start(f32[1,64,64]{2,1,0:T(8,128)S(1)} %copy-done.6), channel_id=1, source_target_pairs={{32,0},{64,32},{96,64},{128,96},{160,128},{192,160},{224,192},{256... | collective-permute-start | bytes 49160 | tf_op jit(solution)/shard_map/ppermute | solution.py:15
  363.9 33.3 %copy-start.4 = (f32[64,64]{1,0:T(8,128)S(1)}, f32[64,64]{1,0:T(8,128)}, u32[]{:S(2)}) copy-start(f32[64,64]{1,0:T(8,128)} %param.11) | copy-start | bytes 49156
  381.4 77.5 %copy-start.2 = (f32[1,64,2048]{2,1,0:T(8,128)S(1)}, f32[1,64,2048]{2,1,0:T(8,128)}, u32[]{:S(2)}) copy-start(f32[1,64,2048]{2,1,0:T(8,128)} %param.8) | copy-start | bytes 1572868
  383.2 70.8 %all-to-all-start.1 = ((f32[32,1,4096]{2,1,0:T(1,128)}), f32[32,1,4096]{2,1,0:T(1,128)S(1)}, u32[]{:S(2)}, u32[]{:S(2)}) async-start(f32[32,1,4096]{2,1,0:T(1,128)} %reshape.19), calls=%async_computation.1 | async-start | bytes 1048576 | tf_op jit(solution)/shard_map/all_to_all | solution.py:45
  454.0 22.6 %copy-start.3 = (f32[64,64]{1,0:T(8,128)}, f32[64,64]{1,0:T(8,128)S(1)}, u32[]{:S(2)}) copy-start(f32[64,64]{1,0:T(8,128)S(1)} %convolution_add_fusion.1) | copy-start | bytes 49156
